TPU v7x, 512 devices: a whole 4x8x8 slice. The times are simulated.
512 devices in a mesh: survey: 16 (over z, core), tile: 32 (over y, x).
Axes of the slice: x: 4, y: 8, z: 8, core: 2. Of those that a mesh axis runs over, the one named last changes fastest.
Arguments:
- data: bfloat16 [16, 256, 128, 256], P('survey', 'tile'), may hold values from -12 to 12
- correlation_index: int32 [16, 32, 16, 128], P(None, 'tile'), may hold values from 0 to 1023, as said below
- correlation_count: int32 [16, 32, 16], P(None, 'tile'), may hold values from 0 to 128, as said below
- smoothing: float32 [3], replicated, may hold values from 0.5 to 4
Outputs:
- fields: float32 [16, 3, 256, 128], P('survey', None, 'tile')
- volume: bfloat16 [16, 256, 128, 256], P('survey', 'tile')
Inputs may be any that keep to these rules, and one draw needn't show every extreme that they name: `correlation_index`: each list holds 128 consecutive positions of the tile. `correlation_count`: zero where s equals p; one or more where s is p + 1 modulo 16; in every draw one tile and one destination group receive 128 live slots from every other group.
All inputs are finite; a program needn't handle non-finite values.
Results may differ from a plain program's by a relative error of at most 0.0014.
Values may be sent and summed in bfloat16 or wider, within the bound.
A program may use at most 64 MiB of HBM per device.

v0:
```python
import jax
import jax.numpy as jnp
from jax import lax
from jax.sharding import PartitionSpec as P

ROUNDS = 2
CG_ITERS = 3


damping = 0.05
sim_eps = 1e-05


def extended(array, sides, width):
    for axis, dim in sides:
        devices, length = (lax.axis_size(axis), array.shape[dim])
        up = [(i, (i + 1) % devices) for i in range(devices - 1)]
        down = [(j, i) for i, j in up]
        last = lax.slice_in_dim(array, length - width, length, axis=dim)
        leading = lax.slice_in_dim(array, 0, width, axis=dim)
        before = lax.ppermute(last, axis, up)
        after = lax.ppermute(leading, axis, down)
        array = jnp.concatenate([before, array, after], axis=dim)
    return array


def time_axis(samples):
    return (jnp.arange(samples, dtype=jnp.float32) - (samples - 1) / 2.0) / (samples / 2.0)


def time_slope(trace_rows):
    padded = jnp.pad(trace_rows, [(0, 0)] * (trace_rows.ndim - 1) + [(1, 1)])
    return 0.5 * (padded[..., 2:] - padded[..., :-2])


def corrected(raw_rows, time_shift, log_gain, gain_trend):
    values = raw_rows.astype(jnp.float32)
    time_pos = time_axis(raw_rows.shape[-1])
    amplitude = jnp.exp(log_gain[..., None] + gain_trend[..., None] * time_pos)
    return (amplitude * (values + time_shift[..., None] * time_slope(values))).astype(jnp.bfloat16)


def pair_terms(own_rows, partner_rows, live_mask):
    own_vals = own_rows.astype(jnp.float32)
    partner_vals = partner_rows.astype(jnp.float32)
    time_pos = time_axis(own_vals.shape[-1])
    residual = partner_vals - own_vals
    moved = time_slope(own_vals)
    tilted = time_pos * own_vals
    energy = jnp.mean(own_vals * own_vals, axis=-1)
    cross_term = jnp.mean(own_vals * partner_vals, axis=-1)
    other_energy = jnp.mean(partner_vals * partner_vals, axis=-1)
    weight = live_mask * cross_term * cross_term / ((energy + sim_eps) * (other_energy + sim_eps))
    numerator = jnp.stack(
        [
            jnp.mean(residual * moved, axis=-1),
            jnp.mean(residual * own_vals, axis=-1),
            jnp.mean(residual * tilted, axis=-1),
        ]
    )
    denominator = jnp.stack(
        [jnp.mean(moved * moved, axis=-1), energy, jnp.mean(tilted * tilted, axis=-1)]
    )
    return (weight * numerator, weight * denominator)


def send_traces(current, send_index):
    outgoing = jnp.take(current, send_index, axis=0)
    return lax.all_to_all(outgoing, "survey", split_axis=0, concat_axis=0, tiled=True)


def smooth_apply(field, weights, strength):
    padded = extended(field, (("tile", 1),), 1)
    padded = jnp.pad(padded, ((0, 0), (0, 0), (1, 1)))
    beside = padded[:, 2:, 1:-1] + padded[:, :-2, 1:-1] + padded[:, 1:-1, 2:] + padded[:, 1:-1, :-2]
    return (weights + damping + 4.0 * strength) * field - strength * beside


def squares(residual):
    return lax.psum(jnp.sum(residual * residual, axis=(1, 2)), "tile")


def conjugate(target, weights, strength):
    solution = jnp.zeros_like(target)
    residual = target
    direction = target
    norm_now = squares(residual)
    for iteration in range(CG_ITERS):
        image = smooth_apply(direction, weights, strength)
        alpha = norm_now / lax.psum(jnp.sum(direction * image, axis=(1, 2)), "tile")
        solution = solution + alpha[:, None, None] * direction
        residual = residual - alpha[:, None, None] * image
        norm_next = squares(residual)
        direction = residual + (norm_next / norm_now)[:, None, None] * direction
        norm_now = norm_next
    return solution


def solve_round(current, partner_rows, recv_index, live_mask, strength, rows_x, rows_y):
    own_rows = jnp.take(current, recv_index, axis=0)
    numerator, denominator = pair_terms(own_rows, partner_rows, live_mask)
    empty_sum = jnp.zeros((3, rows_x * rows_y), jnp.float32)
    target = empty_sum.at[:, recv_index].add(numerator).reshape(3, rows_x, rows_y)
    weights = empty_sum.at[:, recv_index].add(denominator).reshape(3, rows_x, rows_y)
    update = conjugate(target, weights, strength)
    return update.reshape(3, rows_x * rows_y)


def local(data, correlation_index, correlation_count, smoothing):
    own_group = lax.axis_index("survey")
    rows_x, rows_y, samples = (data.shape[1], data.shape[2], data.shape[3])
    flat_data = data.reshape(rows_x * rows_y, samples)
    index_here = correlation_index[:, 0]
    count_here = correlation_count[:, 0]
    send_index = lax.dynamic_index_in_dim(index_here, own_group, axis=0, keepdims=False)
    recv_index = lax.dynamic_index_in_dim(index_here, own_group, axis=1, keepdims=False)
    recv_count = lax.dynamic_index_in_dim(count_here, own_group, axis=1, keepdims=False)
    slot_ids = jnp.arange(index_here.shape[2], dtype=jnp.int32)
    live_mask = (slot_ids[None, :] < recv_count[:, None]).astype(jnp.float32)
    strength = smoothing[:, None, None]
    fields = jnp.zeros((3, rows_x * rows_y), jnp.float32)
    for outer_round in range(ROUNDS):
        current = corrected(flat_data, fields[0], fields[1], fields[2])
        partner_rows = send_traces(current, send_index)
        fields = fields + solve_round(
            current, partner_rows, recv_index, live_mask, strength, rows_x, rows_y
        )
    volume = corrected(flat_data, fields[0], fields[1], fields[2])
    return (fields.reshape(1, 3, rows_x, rows_y), volume.reshape(1, rows_x, rows_y, samples))


def solution(mesh):
    placed = (
        P("survey", "tile", None, None),
        P(None, "tile", None, None),
        P(None, "tile", None),
        P(),
    )
    return jax.shard_map(
        local,
        mesh=mesh,
        in_specs=placed,
        out_specs=(P("survey", None, "tile", None), P("survey", "tile", None, None)),
        check_vma=False,
    )
```

profile of v0, /device:TPU:6, one launch (start us, length us, event | category | flops | bytes accessed | tf_op | source)
XLA Modules:
  0.0 919.4 jit_solution(10757144252853835753)
XLA Ops:
  0.7 0.7 bitcast_clamp_fusion
  1.4 0.7 compare_and_fusion
  2.1 1.1 bitcast_convert_fusion
  3.2 1.7 multiply_convert_fusion.2
  4.9 7.5 gather_fusion.1
  12.4 1.3 broadcast_select_fusion.1
  13.6 10.5 %all-to-all-start = ((bf16[16,128,256]{2,1,0:T(8,128)(2,1)}), bf16[16,128,256]{2,1,0:T(8,128)(2,1)}, u32[]{:S(2)}, u32[]{:S(2)}) async-start(bf16[16,128,256]{2,1,0:T(8,128)(2,1)} %broadcast_select_fusion.1), calls=%async_computation | async-start | bytes 2097152 | tf_op jit(solution)/shard_map/all_to_all | solution.py:69
  24.1 0.9 constant_dynamic-slice_fusion
  25.0 7.5 gather_fusion
  32.5 0.4 dynamic-slice_reduce_fusion
  33.0 1.7 fusion.25
  34.7 16.1 %all-to-all-done = bf16[16,128,256]{2,1,0:T(8,128)(2,1)} async-done(((bf16[16,128,256]{2,1,0:T(8,128)(2,1)}), bf16[16,128,256]{2,1,0:T(8,128)(2,1)}, u32[]{:S(2)}, u32[]{:S(2)}) %all-to-all-start) | async-done | bytes 1048608 | tf_op jit(solution)/shard_map/all_to_all | solution.py:69
  50.8 9.2 %fusion.16 = (f32[16,128]{1,0:T(8,128)S(1)}, f32[16,128]{1,0:T(8,128)S(1)}, f32[16,128]{1,0:T(8,128)S(1)}, f32[16,128]{1,0:T(8,128)S(1)}, f32[16,128]{1,0:T(8,12...) fusion(bf16[16,128,256]{2,1,0:T(8,128)(2,1)} %all-to-all-done, ...), kind=kLoop, calls=%fused_computation.40 | loop fusion | flops 13090816 | bytes 4262912 | tf_op jit(solution)/shard_map/reduce_sum | solution.py:51
  60.2 0.4 copy.60
  60.5 11.6 %scatter_custom_fusion = f32[3,1024]{0,1:T(8,128)S(1)} fusion(s32[2048]{0:T(1024)S(1)} %fusion.64, f32[2048,3]{1,0:T(8,128)S(1)} %bitcast.90, f32[]{:T(128)} %constant.66.clone.1), kind=kCustom, calls=%fused_computation.71 | custom fusion | flops 6144 | bytes 12292 | tf_op jit(solution)/shard_map/scatter-add | solution.py:103
  72.2 0.2 copy.43
  72.3 2.7 collective-permute-start
  75.1 5.2 collective-permute-start.1
  80.5 0.4 copy.61
  80.8 11.6 %scatter_custom_fusion.1 = f32[3,1024]{0,1:T(8,128)S(1)} fusion(s32[2048]{0:T(1024)S(1)} %fusion.64, f32[2048,3]{1,0:T(8,128)S(1)} %bitcast.91, f32[]{:T(128)} %constant.77.clone.1), kind=kCustom, calls=%fused_computation.67 | custom fusion | flops 6144 | bytes 12292 | tf_op jit(solution)/shard_map/scatter-add | solution.py:104
  92.4 0.2 copy.36
  92.9 65.2 %all-reduce.10 = (f32[3]{0:T(128)S(1)}, f32[3]{0:T(128)S(1)}) all-reduce(f32[3]{0:T(128)S(1)} %multiply_reduce_fusion.3, f32[3]{0:T(128)S(1)} %multiply_reduce_fusion.11), channel_id=1, replica_groups=mesh['survey'=16,'tile'=32] {'tile'}, use_global_device_ids=true, to_apply=%region_8.10 | all-reduce | flops 6 | bytes 48 | tf_op jit(solution)/shard_map/psum | solution.py:80
  158.1 0.2 multiply_reduce_fusion.10
  158.3 72.3 %psum.86 = f32[3]{0:T(128)S(1)} all-reduce(f32[3]{0:T(128)S(1)} %get-tuple-element.29), channel_id=1, replica_groups=mesh['survey'=16,'tile'=32] {'tile'}, use_global_device_ids=true, to_apply=%region_15.17 | all-reduce | flops 3 | bytes 24 | tf_op jit(solution)/shard_map/psum | solution.py:80
  230.7 1.9 collective-permute-start.2
  232.6 6.0 collective-permute-start.3
  238.7 2.7 collective-permute-done.3
  241.5 0.2 multiply_reduce_fusion.9
  241.7 66.0 %psum.87 = f32[3]{0:T(128)S(1)} all-reduce(f32[3]{0:T(128)S(1)} %get-tuple-element.27), channel_id=1, replica_groups=mesh['survey'=16,'tile'=32] {'tile'}, use_global_device_ids=true, to_apply=%region_17.19 | all-reduce | flops 3 | bytes 24 | tf_op jit(solution)/shard_map/psum | solution.py:90
  307.9 71.9 %psum.88 = f32[3]{0:T(128)S(1)} all-reduce(f32[3]{0:T(128)S(1)} %multiply_reduce_fusion.8), channel_id=1, replica_groups=mesh['survey'=16,'tile'=32] {'tile'}, use_global_device_ids=true, to_apply=%region_19.21 | all-reduce | flops 3 | bytes 24 | tf_op jit(solution)/shard_map/psum | solution.py:80
  379.9 2.0 collective-permute-start.4
  381.9 6.0 collective-permute-start.5
  387.9 2.7 collective-permute-done.5
  390.9 66.3 %psum.89 = f32[3]{0:T(128)S(1)} all-reduce(f32[3]{0:T(128)S(1)} %fusion.54), channel_id=1, replica_groups=mesh['survey'=16,'tile'=32] {'tile'}, use_global_device_ids=true, to_apply=%region_21.23 | all-reduce | flops 3 | bytes 24 | tf_op jit(solution)/shard_map/psum | solution.py:90
  457.2 1.0 multiply_convert_fusion.1
  458.3 7.5 gather_fusion.3
  465.8 1.3 broadcast_select_fusion
  467.1 4.9 all-to-all-start.1
  471.9 7.5 gather_fusion.2
  479.4 1.7 fusion.26
  481.1 17.5 %all-to-all-done.1 = bf16[16,128,256]{2,1,0:T(8,128)(2,1)} async-done(((bf16[16,128,256]{2,1,0:T(8,128)(2,1)}), bf16[16,128,256]{2,1,0:T(8,128)(2,1)}, u32[]{:S(2)}, u32[]{:S(2)}) %all-to-all-start.1) | async-done | bytes 1048608 | tf_op jit(solution)/shard_map/all_to_all | solution.py:69
  498.6 9.2 %fusion.18 = (f32[16,128]{1,0:T(8,128)S(1)}, f32[16,128]{1,0:T(8,128)S(1)}, f32[16,128]{1,0:T(8,128)S(1)}, f32[16,128]{1,0:T(8,128)S(1)}, f32[16,128]{1,0:T(8,12...) fusion(bf16[16,128,256]{2,1,0:T(8,128)(2,1)} %all-to-all-done.1, ...), kind=kLoop, calls=%fused_computation.42 | loop fusion | flops 13090816 | bytes 4262912 | tf_op jit(solution)/shard_map/reduce_sum | solution.py:51
  508.0 0.4 copy.62
  508.4 11.6 %scatter_custom_fusion.2 = f32[3,1024]{0,1:T(8,128)S(1)} fusion(s32[2048]{0:T(1024)S(1)} %fusion.64, f32[2048,3]{1,0:T(8,128)S(1)} %bitcast.89, f32[]{:T(128)} %constant.66.clone.1), kind=kCustom, calls=%fused_computation.69 | custom fusion | flops 6144 | bytes 12292 | tf_op jit(solution)/shard_map/scatter-add | solution.py:103
  520.0 0.2 copy.56
  520.1 4.2 collective-permute-start.6
  524.3 3.8 collective-permute-start.7
  528.3 0.4 copy.63
  528.6 11.6 %scatter_custom_fusion.3 = f32[3,1024]{0,1:T(8,128)S(1)} fusion(s32[2048]{0:T(1024)S(1)} %fusion.64, f32[2048,3]{1,0:T(8,128)S(1)} %bitcast.88, f32[]{:T(128)} %constant.77.clone.1), kind=kCustom, calls=%fused_computation.65 | custom fusion | flops 6144 | bytes 12292 | tf_op jit(solution)/shard_map/scatter-add | solution.py:104
  540.2 0.2 copy.49
  540.7 69.8 %all-reduce.9 = (f32[3]{0:T(128)S(1)}, f32[3]{0:T(128)S(1)}) all-reduce(f32[3]{0:T(128)S(1)} %multiply_reduce_fusion.2, f32[3]{0:T(128)S(1)} %multiply_reduce_fusion.7), channel_id=1, replica_groups=mesh['survey'=16,'tile'=32] {'tile'}, use_global_device_ids=true, to_apply=%region_30.32 | all-reduce | flops 6 | bytes 48 | tf_op jit(solution)/shard_map/psum | solution.py:80
  610.5 0.2 multiply_reduce_fusion.6
  610.7 71.5 %psum.92 = f32[3]{0:T(128)S(1)} all-reduce(f32[3]{0:T(128)S(1)} %get-tuple-element.25), channel_id=1, replica_groups=mesh['survey'=16,'tile'=32] {'tile'}, use_global_device_ids=true, to_apply=%region_37.39 | all-reduce | flops 3 | bytes 24 | tf_op jit(solution)/shard_map/psum | solution.py:80
  682.3 2.1 collective-permute-start.8
  684.3 5.9 collective-permute-start.9
  690.2 1.3 collective-permute-done.9
  691.6 0.2 multiply_reduce_fusion.5
  691.8 73.1 %psum.93 = f32[3]{0:T(128)S(1)} all-reduce(f32[3]{0:T(128)S(1)} %get-tuple-element.23), channel_id=1, replica_groups=mesh['survey'=16,'tile'=32] {'tile'}, use_global_device_ids=true, to_apply=%region_39.41 | all-reduce | flops 3 | bytes 24 | tf_op jit(solution)/shard_map/psum | solution.py:90
  765.1 69.6 %psum.94 = f32[3]{0:T(128)S(1)} all-reduce(f32[3]{0:T(128)S(1)} %multiply_reduce_fusion.4), channel_id=1, replica_groups=mesh['survey'=16,'tile'=32] {'tile'}, use_global_device_ids=true, to_apply=%region_41.43 | all-reduce | flops 3 | bytes 24 | tf_op jit(solution)/shard_map/psum | solution.py:80
  834.8 1.9 collective-permute-start.10
  836.7 6.0 collective-permute-start.11
  842.8 1.3 collective-permute-done.11
  844.3 73.1 %psum.95 = f32[3]{0:T(128)S(1)} all-reduce(f32[3]{0:T(128)S(1)} %fusion.43), channel_id=1, replica_groups=mesh['survey'=16,'tile'=32] {'tile'}, use_global_device_ids=true, to_apply=%region_43.45 | all-reduce | flops 3 | bytes 24 | tf_op jit(solution)/shard_map/psum | solution.py:90
  917.5 1.8 multiply_convert_fusion
  (72 shorter events, 2.8 us)
Async XLA Ops:
  0.6 31.9 %copy-start = (s32[16,1,16]{2,1,0:T(1,128)S(1)}, s32[16,1,16]{2,1,0:T(1,128)}, u32[]{:S(2)}) copy-start(s32[16,1,16]{2,1,0:T(1,128)} %param.8) | copy-start | bytes 3076
  13.6 37.2 %all-to-all-start = ((bf16[16,128,256]{2,1,0:T(8,128)(2,1)}), bf16[16,128,256]{2,1,0:T(8,128)(2,1)}, u32[]{:S(2)}, u32[]{:S(2)}) async-start(bf16[16,128,256]{2,1,0:T(8,128)(2,1)} %broadcast_select_fusion.1), calls=%async_computation | async-start | bytes 2097152 | tf_op jit(solution)/shard_map/all_to_all | solution.py:69
  25.0 8.0 copy-start.3
  60.5 396.7 %copy-start.1 = (bf16[1,8,128,256]{3,2,1,0:T(8,128)(2,1)S(1)}, bf16[1,8,128,256]{3,2,1,0:T(8,128)(2,1)}, u32[]{:S(2)}) copy-start(bf16[1,8,128,256]{3,2,1,0:T(8,128)(2,1)} %param.6) | copy-start | bytes 1572868
  72.3 20.3 %collective-permute-start = (f32[3,1,128]{2,1,0:T(1,128)S(1)}, f32[3,1,128]{2,1,0:T(1,128)S(1)}, u32[]{:S(2)}, u32[]{:S(2)}) collective-permute-start(f32[3,1,128]{2,1,0:T(1,128)S(1)} %get-tuple-element.48), channel_id=1, source_target_pairs={{1,0},{2,1},{3,2},{4,3},{5,4},{6,5},{7,6},{8,7},{9,8},{10,9},{11,1... | collective-permute-start | bytes 4616 | tf_op jit(solution)/shard_map/ppermute | solution.py:22
  75.1 17.5 %collective-permute-start.1 = (f32[3,1,128]{2,1,0:T(1,128)S(1)}, f32[3,1,128]{2,1,0:T(1,128)S(1)}, u32[]{:S(2)}, u32[]{:S(2)}) collective-permute-start(f32[3,1,128]{2,1,0:T(1,128)S(1)} %get-tuple-element.47), channel_id=1, source_target_pairs={{0,1},{1,2},{2,3},{3,4},{4,5},{5,6},{6,7},{7,8},{8,9},{9,10},{10,1... | collective-permute-start | bytes 4616 | tf_op jit(solution)/shard_map/ppermute | solution.py:21
  230.7 8.0 collective-permute-start.2
  232.6 8.8 collective-permute-start.3
  379.9 8.0 collective-permute-start.4
  381.9 8.7 collective-permute-start.5
  467.1 31.6 %all-to-all-start.1 = ((bf16[16,128,256]{2,1,0:T(8,128)(2,1)}), bf16[16,128,256]{2,1,0:T(8,128)(2,1)}, u32[]{:S(2)}, u32[]{:S(2)}) async-start(bf16[16,128,256]{2,1,0:T(8,128)(2,1)} %broadcast_select_fusion), calls=%async_computation.1 | async-start | bytes 2097152 | tf_op jit(solution)/shard_map/all_to_all | solution.py:69
  520.1 20.3 %collective-permute-start.6 = (f32[3,1,128]{2,1,0:T(1,128)S(1)}, f32[3,1,128]{2,1,0:T(1,128)S(1)}, u32[]{:S(2)}, u32[]{:S(2)}) collective-permute-start(f32[3,1,128]{2,1,0:T(1,128)S(1)} %get-tuple-element.39), channel_id=1, source_target_pairs={{1,0},{2,1},{3,2},{4,3},{5,4},{6,5},{7,6},{8,7},{9,8},{10,9},{11,1... | collective-permute-start | bytes 4616 | tf_op jit(solution)/shard_map/ppermute | solution.py:22
  524.3 16.1 %collective-permute-start.7 = (f32[3,1,128]{2,1,0:T(1,128)S(1)}, f32[3,1,128]{2,1,0:T(1,128)S(1)}, u32[]{:S(2)}, u32[]{:S(2)}) collective-permute-start(f32[3,1,128]{2,1,0:T(1,128)S(1)} %get-tuple-element.38), channel_id=1, source_target_pairs={{0,1},{1,2},{2,3},{3,4},{4,5},{5,6},{6,7},{7,8},{8,9},{9,10},{10,1... | collective-permute-start | bytes 4616 | tf_op jit(solution)/shard_map/ppermute | solution.py:21
  682.3 8.0 collective-permute-start.8
  684.3 7.2 collective-permute-start.9
  834.8 8.0 collective-permute-start.10
  836.7 7.3 collective-permute-start.11
  917.5 1.9 copy-start.2
where the time goes:
time: 937 us; the launch traced here: 919 us
  blocking collectives  699 us (75%)
  other arithmetic  81.2 us (9%)
  starting transfers between devices  63 us (7%)
  waiting for transfers between devices  41.7 us (4%)
  local copies, waits for them, and re-layouts  33.5 us (4%)
    psum x6, blocking collectives, squares(): return lax.psum(jnp.sum(residual * residual, axis=(1, 2)), 'tile')  420 us
    psum x4, blocking collectives, conjugate(): alpha = norm_now / lax.psum(jnp.sum(direction * image, axis=(1, 2)), 'tile')  279 us
    all_to_all x2, waiting for transfers between devices, send_traces(): lax.all_to_all(outgoing, 'survey', split_axis=0, concat_axis=0, tiled=True)  33.6 us
    ppermute x6, starting transfers between devices, extended(): before = lax.ppermute(last, axis, up)  32.9 us
    scatter-add x2, other arithmetic, solve_round(): empty_sum.at[:, recv_index].add(denominator).reshape(3, rows_x, rows_y)  23.2 us
    scatter-add x2, other arithmetic, solve_round(): empty_sum.at[:, recv_index].add(numerator).reshape(3, rows_x, rows_y)  23.2 us
  transfers between devices with their start and end apart: 14, of which 6 were waited for; matrix products, arithmetic and copies ran while one was open for 5% of the time, Pallas kernels for 0%

commit v1 on v0

v1 whole, which is shorter than its diff:
```python
import functools

import jax
import jax.numpy as jnp
from jax import lax
from jax.experimental import pallas as pl
from jax.experimental.pallas import tpu as pltpu
from jax.sharding import PartitionSpec as P

ROUNDS = 2
DAMPING = 0.05
SIM_EPS = 1e-05
CG_ITERS = 3
CHUNK = 32
LANES = 128
F32 = jnp.float32
BF16 = jnp.bfloat16


def slope_of(v):
    n = v.shape[0]
    row = lax.broadcasted_iota(jnp.int32, v.shape, 0)
    after = jnp.where(row == n - 1, 0.0, pltpu.roll(v, n - 1, 0))
    before = jnp.where(row == 0, 0.0, pltpu.roll(v, 1, 0))
    return 0.5 * (after - before)


def time_rows(start, length, samples):
    row = lax.broadcasted_iota(jnp.int32, (length, LANES), 0) + start
    return (row.astype(F32) - (samples - 1) / 2.0) / (samples / 2.0)


def fold(a):
    return jnp.sum(a.reshape(a.shape[0] // 8, 8, a.shape[1]), axis=0)


def kernel(
    survey_n, tile_n, data_hbm, index_hbm, count_hbm, strength_hbm, fields_ref,
    data, send_index, recv_index, count_ref, strength_ref, raw, raw_slope, own, own_slope, stats,
    out_lists, in_lists, list_raw, list_slope,
    edge_out, edge_low, edge_high, moment_out, moment_in, field_rows, field_out, field_in,
    load_sem, list_send, list_recv, edge_send, edge_recv, moment_send, moment_recv, field_send, field_recv,
):
    rows_x, rows_y, samples = data.shape
    me = lax.axis_index("survey")
    tile = lax.axis_index("tile")
    peers = survey_n - 1
    others = tile_n - 1
    lane = lax.broadcasted_iota(jnp.int32, (8, LANES), 1)
    sub = lax.broadcasted_iota(jnp.int32, (8, LANES), 0)
    lane1 = lax.broadcasted_iota(jnp.int32, (1, LANES), 1)

    def offset(j):
        half = (j + 1) // 2
        return jnp.where(j % 2 == 0, half + 1, survey_n - half)

    def receiver(j):
        return lax.rem(me + offset(j), survey_n)

    def sender(j):
        return lax.rem(me + survey_n - offset(j), survey_n)

    loads = [
        pltpu.make_async_copy(index_hbm.at[me, 0], send_index, load_sem.at[0]),
        pltpu.make_async_copy(data_hbm.at[0], data, load_sem.at[1]),
        pltpu.make_async_copy(index_hbm.at[:, 0, me], recv_index, load_sem.at[2]),
        pltpu.make_async_copy(count_hbm, count_ref, load_sem.at[3]),
        pltpu.make_async_copy(strength_hbm, strength_ref, load_sem.at[4]),
    ]
    for load in loads:
        load.start()
    barrier = pltpu.get_barrier_semaphore()

    def greet_survey(i, c):
        pl.semaphore_signal(barrier, inc=1, device_id={"survey": lax.rem(me + i, survey_n)},
                            device_id_type=pl.DeviceIdType.MESH)
        return c

    def greet_tile(i, c):
        pl.semaphore_signal(barrier, inc=1, device_id={"tile": lax.rem(tile + i, tile_n)},
                            device_id_type=pl.DeviceIdType.MESH)
        return c

    lax.fori_loop(1, survey_n, greet_survey, 0)
    lax.fori_loop(1, tile_n, greet_tile, 0)
    loads[0].wait()
    loads[1].wait()

    def list_copy(j):
        return pltpu.make_async_remote_copy(
            src_ref=out_lists.at[j], dst_ref=in_lists.at[j], send_sem=list_send.at[j],
            recv_sem=list_recv.at[j], device_id={"survey": receiver(j)},
            device_id_type=pl.DeviceIdType.MESH)

    def build_list(j):
        start = send_index[receiver(j), 0]
        x0 = start // LANES
        y0 = start % LANES
        x1 = jnp.minimum(x0 + 1, rows_x - 1)
        for y in range(0, rows_y, CHUNK):
            place = lax.broadcasted_iota(jnp.int32, (CHUNK, samples), 0) + y
            first = place.astype(F32).astype(BF16) >= jnp.full((CHUNK, samples), y0, jnp.int32).astype(F32).astype(BF16)
            out_lists[j, y:y + CHUNK, :] = jnp.where(first, data[x0, y:y + CHUNK, :], data[x1, y:y + CHUNK, :])

    build_list(0)
    pl.semaphore_wait(barrier, peers + others)
    list_copy(0).start()

    def send_list(j, c):
        build_list(j)
        list_copy(j).start()
        return c

    lax.fori_loop(1, peers, send_list, 0)
    for load in loads[2:]:
        load.wait()

    def row_stats(x, slopes, values):
        sums = [jnp.zeros((8, LANES), F32) for _ in range(5)]
        for t in range(0, samples, CHUNK):
            u = values[x, t:t + CHUNK, :].astype(F32)
            a = slopes[x, t:t + CHUNK, :]
            w = u * time_rows(t, CHUNK, samples)
            for k, (p, q) in enumerate(((u, u), (a, a), (w, w), (u, a), (u, w))):
                sums[k] = sums[k] + fold(p * q)
        for k in range(5):
            stats[k, pl.ds(x, 1), :] = jnp.sum(sums[k], axis=0, keepdims=True) * (1.0 / samples)

    def first_own(x, c):
        raw[x] = data[x].T
        raw_slope[x] = slope_of(raw[x].astype(F32))
        row_stats(x, raw_slope, raw)
        return c

    lax.fori_loop(0, rows_x, first_own, 0)

    def later_own(x, c):
        shift = fields_ref[0, 0, pl.ds(x, 1), :]
        log_gain = fields_ref[0, 1, pl.ds(x, 1), :]
        trend = fields_ref[0, 2, pl.ds(x, 1), :]
        for t in range(0, samples, CHUNK):
            amplitude = jnp.exp(log_gain + trend * time_rows(t, CHUNK, samples))
            d = raw[x, t:t + CHUNK, :].astype(F32)
            own[x, t:t + CHUNK, :] = (amplitude * (d + shift * raw_slope[x, t:t + CHUNK, :])).astype(BF16)
        own_slope[x] = slope_of(own[x].astype(F32))
        row_stats(x, own_slope, own)
        return c

    def list_terms(j, carry, values, slopes, partner):
        total, t0, t1, t2 = carry
        source = sender(j)
        start = recv_index[source, 0]
        count = count_ref[source, 0, me]
        x0 = start // LANES
        y0 = start % LANES
        x1 = jnp.minimum(x0 + 1, rows_x - 1)
        y = lax.broadcasted_iota(jnp.int32, (CHUNK, LANES), 1)
        first = y >= y0
        sums = [jnp.zeros((8, LANES), F32) for _ in range(4)]
        for t in range(0, samples, CHUNK):
            v = partner(j, t)
            u = jnp.where(first, values[x0, t:t + CHUNK, :], values[x1, t:t + CHUNK, :]).astype(F32)
            a = jnp.where(first, slopes[x0, t:t + CHUNK, :], slopes[x1, t:t + CHUNK, :])
            uv = u * v
            sums[0] = sums[0] + fold(uv)
            sums[1] = sums[1] + fold(a * v)
            sums[2] = sums[2] + fold(uv * time_rows(t, CHUNK, samples))
            sums[3] = sums[3] + fold(v * v)
        uv, av, wv, vv = [jnp.sum(s, axis=0, keepdims=True) * (1.0 / samples) for s in sums]
        slot = sub * LANES + lane - start
        live = (slot >= 0) & (slot < count)
        uu = stats[0]
        weight = jnp.where(live, (uv * uv) / ((uu + SIM_EPS) * (vv + SIM_EPS)), 0.0)
        return (total + weight, t0 + weight * (av - stats[3]), t1 + weight * (uv - uu),
                t2 + weight * (wv - stats[4]))

    def first_list(j, carry):
        list_copy(j).wait_recv()
        d = in_lists[j].T
        list_raw[j] = d
        return list_terms(j, carry, raw, raw_slope, lambda j, t: list_raw[j, t:t + CHUNK, :].astype(F32))

    def later_partner(j, t):
        shift = field_in[j, 0:1, :]
        log_gain = field_in[j, 1:2, :]
        trend = field_in[j, 2:3, :]
        amplitude = jnp.exp(log_gain + trend * time_rows(t, CHUNK, samples))
        d = list_raw[j, t:t + CHUNK, :].astype(F32)
        return (amplitude * (d + shift * list_slope[j, t:t + CHUNK, :])).astype(BF16).astype(F32)

    def field_copy(j):
        return pltpu.make_async_remote_copy(
            src_ref=field_out.at[j], dst_ref=field_in.at[j], send_sem=field_send.at[j],
            recv_sem=field_recv.at[j], device_id={"survey": receiver(j)},
            device_id_type=pl.DeviceIdType.MESH)

    def later_list(j, carry):
        field_copy(j).wait_recv()
        return list_terms(j, carry, own, own_slope, later_partner)

    def send_fields(i, c):
        j = peers - 1 - i
        start = send_index[receiver(j), 0]
        x0 = start // LANES
        y0 = start % LANES
        x1 = jnp.minimum(x0 + 1, rows_x - 1)
        field_out[j] = jnp.where(lane >= y0, field_rows[x0], field_rows[x1])
        field_copy(j).start()
        return c

    def edge_copy(side, r):
        step = 1 if side == 0 else tile_n - 1
        return pltpu.make_async_remote_copy(
            src_ref=edge_out.at[r], dst_ref=(edge_low if side == 0 else edge_high).at[r],
            send_sem=edge_send.at[r, side], recv_sem=edge_recv.at[r, side],
            device_id={"tile": lax.rem(tile + step, tile_n)}, device_id_type=pl.DeviceIdType.MESH)

    def moment_copy(r, d):
        return pltpu.make_async_remote_copy(
            src_ref=moment_out.at[r], dst_ref=moment_in.at[r, d],
            send_sem=moment_send.at[r], recv_sem=moment_recv.at[r],
            device_id={"tile": lax.rem(tile + d, tile_n)}, device_id_type=pl.DeviceIdType.MESH)

    def moment_all(r):
        return pltpu.make_async_remote_copy(
            src_ref=moment_in.at[r, pl.ds(1, others)], dst_ref=moment_in.at[r, pl.ds(1, others)],
            send_sem=moment_send.at[r], recv_sem=moment_recv.at[r],
            device_id={"tile": lax.rem(tile + 1, tile_n)}, device_id_type=pl.DeviceIdType.MESH)

    def slope_list(j, c):
        list_slope[j] = slope_of(list_raw[j].astype(F32))
        return c

    def solve(r, total, t0, t1, t2):
        for c, t in enumerate((t0, t1, t2)):
            edge_out[r, c] = t
        edge_out[r, 3] = total * stats[1]
        edge_out[r, 4] = total * stats[0]
        edge_out[r, 5] = total * stats[2]
        edge_copy(0, r).start()
        edge_copy(1, r).start()
        if r == 0:
            lax.fori_loop(0, peers, slope_list, 0)
        edge_copy(0, r).wait_recv()
        edge_copy(1, r).wait_recv()

        row = lax.broadcasted_iota(jnp.int32, (24, LANES), 0)
        col = lax.broadcasted_iota(jnp.int32, (24, LANES), 1)
        inside = ((row >= 8) | (tile > 0)) & ((row < 16) | (tile < tile_n - 1))
        state = []
        for c in range(3):
            strength = strength_ref[c]
            b = jnp.where(inside, jnp.concatenate([edge_low[r, c], edge_out[r, c], edge_high[r, c]], axis=0), 0.0)
            w = jnp.where(inside, jnp.concatenate(
                [edge_low[r, 3 + c], edge_out[r, 3 + c], edge_high[r, 3 + c]], axis=0), 0.0)
            bound = jnp.max(jnp.max(w, axis=0, keepdims=True), axis=1, keepdims=True) + (DAMPING + 8.0 * strength)
            scale = 1.0 / bound
            diagonal = (w + DAMPING + 4.0 * strength) * scale
            state.append([b, b, None, bound, diagonal, strength * scale])

        def apply(y, diagonal, off):
            up = pltpu.roll(y, 1, 0)
            down = pltpu.roll(y, 23, 0)
            left = jnp.where(col == 0, 0.0, pltpu.roll(y, 1, 1))
            right = jnp.where(col == LANES - 1, 0.0, pltpu.roll(y, LANES - 1, 1))
            return jnp.where(inside, diagonal * y - off * (up + down + left + right), 0.0)

        power = lane1 % 8

        def powers(q):
            return jnp.where(power == 1, q, 1.0) * jnp.where(power == 2, q * q, 1.0)

        for step in range(CG_ITERS):
            slot = r * CG_ITERS + step
            message = jnp.where(lane1 >= 64, 1.0, 0.0).astype(F32)
            images = []
            for c in range(3):
                residual, direction, update, bound, diagonal, off = state[c]
                image = apply(direction, diagonal, off)
                images.append(image)
                p0, p1, q1 = residual[8:16], direction[8:16], image[8:16]
                block = jnp.zeros((8, LANES), F32)
                for k, (p, q) in enumerate(((p0, p0), (p1, q1), (q1, q1))):
                    block = jnp.where(sub == k, jnp.sum(p * q, axis=0, keepdims=True), block)
                sums = jnp.sum(block, axis=1, keepdims=True)
                message = message + jnp.sum(jnp.where(lane == 8 * c + sub, sums, 0.0), axis=0, keepdims=True)
                message = jnp.where((lane1 >= 64 + 8 * c) & (lane1 < 72 + 8 * c), bound, message)
            moment_out[slot] = message
            moment_in[slot, 0] = message

            def send_moments(i, c):
                half = (i + 1) // 2
                moment_copy(slot, tile_n // 2 + jnp.where(i % 2 == 0, half, -half)).start()
                return c

            lax.fori_loop(0, others, send_moments, 0)
            moment_all(slot).wait_recv()
            rows = [moment_in[slot, d] for d in range(tile_n)]
            bounds = [pltpu.roll(m, 64, 1) for m in rows]
            top = functools.reduce(jnp.maximum, bounds)
            inverse = 1.0 / top
            m0 = jnp.zeros((1, LANES), F32)
            for d in range(tile_n):
                m0 = m0 + rows[d] * powers(bounds[d] * inverse)
            m1, m2 = [pltpu.roll(m0, LANES - k, 1) for k in (1, 2)]
            alpha = m0 / m1
            beta = jnp.maximum(alpha * alpha * m2 - m0, 0.0) / m0
            along = alpha * inverse
            back = alpha * inverse * bounds[0]
            for c in range(3):
                k1, k2, k3 = [jnp.sum(jnp.where(lane1 == 8 * c, z, 0.0), axis=1, keepdims=True)
                              for z in (along, back, beta)]
                residual, direction, update = state[c][:3]
                part = k1 * direction[8:16]
                state[c][2] = part if step == 0 else update + part
                state[c][0] = residual - k2 * images[c]
                state[c][1] = state[c][0] + k3 * direction
        for c in range(3):
            fields_ref[0, c] = state[c][2] if r == 0 else fields_ref[0, c] + state[c][2]

    zero = jnp.zeros((8, LANES), F32)
    carry = lax.fori_loop(0, peers, first_list, (zero,) * 4)
    solve(0, *carry)
    for x in range(rows_x):
        for c in range(3):
            field_rows[x, c:c + 1, :] = fields_ref[0, c, x:x + 1, :]
        field_rows[x, 3:8, :] = jnp.zeros((5, LANES), F32)
    lax.fori_loop(0, peers, send_fields, 0)
    lax.fori_loop(0, rows_x, later_own, 0)
    carry = lax.fori_loop(0, peers, later_list, (zero,) * 4)
    solve(1, *carry)

    def drain(j, c):
        list_copy(j).wait_send()
        field_copy(j).wait_send()
        return c

    lax.fori_loop(0, peers, drain, 0)
    for r in range(ROUNDS):
        edge_copy(0, r).wait_send()
        edge_copy(1, r).wait_send()
        for step in range(CG_ITERS):
            moment_all(r * CG_ITERS + step).wait_send()


def correct_kernel(data_hbm, fields_hbm, fields_out, volume_hbm, data, fields, volume, load_sem, store_sem):
    rows_x, rows_y, samples = data.shape
    parts = load_sem.shape[0] - 1
    rows = rows_x // parts
    lane = lax.broadcasted_iota(jnp.int32, (rows_y, samples), 1)
    time_pos = (lane.astype(F32) - (samples - 1) / 2.0) / (samples / 2.0)
    field_load = pltpu.make_async_copy(fields_hbm, fields, load_sem.at[parts])
    field_load.start()

    def load(k):
        part = pl.ds(k * rows, rows)
        return pltpu.make_async_copy(data_hbm.at[0, part], data.at[part], load_sem.at[k])

    def store(k):
        part = pl.ds(k * rows, rows)
        return pltpu.make_async_copy(volume.at[part], volume_hbm.at[0, part], store_sem.at[k])

    for k in range(parts):
        load(k).start()
    field_load.wait()
    field_store = pltpu.make_async_copy(fields, fields_out, store_sem.at[parts])
    field_store.start()
    columns = [fields[0, c].T for c in range(3)]
    for k in range(parts):
        load(k).wait()
        for x in range(k * rows, (k + 1) * rows):
            shift, log_gain, trend = [column[:, x:x + 1] for column in columns]
            d = data[x].astype(F32)
            after = jnp.where(lane == samples - 1, 0.0, pltpu.roll(d, samples - 1, 1))
            before = jnp.where(lane == 0, 0.0, pltpu.roll(d, 1, 1))
            amplitude = jnp.exp(log_gain + trend * time_pos)
            volume[x] = (amplitude * (d + shift * (0.5 * (after - before)))).astype(BF16)
        store(k).start()
    for k in range(parts):
        store(k).wait()
    field_store.wait()


def correct(data, fields):
    rows_x, rows_y, samples = data.shape[1:]
    parts = 4
    block = pltpu.VMEM((rows_x, rows_y, samples), BF16)
    return pl.pallas_call(
        correct_kernel,
        out_shape=(jax.ShapeDtypeStruct(fields.shape, F32), jax.ShapeDtypeStruct(data.shape, BF16)),
        in_specs=[pl.BlockSpec(memory_space=pl.ANY)] * 2,
        out_specs=[pl.BlockSpec(memory_space=pl.ANY)] * 2,
        scratch_shapes=[block, pltpu.VMEM(fields.shape, F32), block,
                        pltpu.SemaphoreType.DMA((parts + 1,)), pltpu.SemaphoreType.DMA((parts + 1,))],
        compiler_params=pltpu.CompilerParams(vmem_limit_bytes=60 * 1024 * 1024),
    )(data, fields)


def local(data, correlation_index, correlation_count, smoothing):
    survey_n = lax.axis_size("survey")
    tile_n = lax.axis_size("tile")
    rows_x, rows_y, samples = data.shape[1:]
    peers = survey_n - 1
    block = (samples, LANES)
    turned = (LANES, samples)
    dma = pltpu.SemaphoreType.DMA
    fields = pl.pallas_call(
        functools.partial(kernel, survey_n, tile_n),
        out_shape=jax.ShapeDtypeStruct((1, 3, rows_x, rows_y), F32),
        in_specs=[pl.BlockSpec(memory_space=pl.ANY)] * 4,
        out_specs=pl.BlockSpec(memory_space=pltpu.VMEM),
        scratch_shapes=[
            pltpu.VMEM((rows_x,) + turned, BF16),
            pltpu.SMEM((survey_n, correlation_index.shape[3]), jnp.int32),
            pltpu.SMEM((survey_n, correlation_index.shape[3]), jnp.int32),
            pltpu.SMEM(correlation_count.shape, jnp.int32),
            pltpu.SMEM(smoothing.shape, F32),
            pltpu.VMEM((rows_x,) + block, BF16),
            pltpu.VMEM((rows_x,) + block, F32),
            pltpu.VMEM((rows_x,) + block, BF16),
            pltpu.VMEM((rows_x,) + block, F32),
            pltpu.VMEM((5, rows_x, LANES), F32),
            pltpu.VMEM((peers,) + turned, BF16),
            pltpu.VMEM((peers,) + turned, BF16),
            pltpu.VMEM((peers,) + block, BF16),
            pltpu.VMEM((peers,) + block, F32),
            pltpu.VMEM((ROUNDS, 6, rows_x, LANES), F32),
            pltpu.VMEM((ROUNDS, 6, rows_x, LANES), F32),
            pltpu.VMEM((ROUNDS, 6, rows_x, LANES), F32),
            pltpu.VMEM((ROUNDS * CG_ITERS, 1, LANES), F32),
            pltpu.VMEM((ROUNDS * CG_ITERS, tile_n, 1, LANES), F32),
            pltpu.VMEM((rows_x, 8, LANES), F32),
            pltpu.VMEM((peers, 8, LANES), F32),
            pltpu.VMEM((peers, 8, LANES), F32),
            dma((5,)),
            dma((peers,)), dma((peers,)),
            dma((ROUNDS, 2)), dma((ROUNDS, 2)),
            dma((ROUNDS * CG_ITERS,)), dma((ROUNDS * CG_ITERS,)),
            dma((peers,)), dma((peers,)),
        ],
        compiler_params=pltpu.CompilerParams(
            collective_id=0, has_side_effects=True, vmem_limit_bytes=60 * 1024 * 1024),
    )(data, correlation_index, correlation_count, smoothing)
    return correct(data, fields)


def solution(mesh):
    placed = (
        P("survey", "tile", None, None),
        P(None, "tile", None, None),
        P(None, "tile", None),
        P(),
    )
    return jax.shard_map(
        local,
        mesh=mesh,
        in_specs=placed,
        out_specs=(P("survey", None, "tile", None), P("survey", "tile", None, None)),
        check_vma=False,
    )
```

time: 937 us -> 96.2 us (0.10); the launches traced: 919 us -> 96 us
  blocking collectives: 699 us -> 0 us
  Pallas kernels: 0 us -> 95.3 us
  other arithmetic: 81.2 us -> 0 us
  starting transfers between devices: 63 us -> 0 us
  waiting for transfers between devices: 41.7 us -> 0 us
  local copies, waits for them, and re-layouts: 33.5 us -> 0 us
    psum x10 -> x0, blocking collectives: 699 us -> none  [the longest x6 420 us: squares(): return lax.psum(jnp.sum(residual * residual, axis=(1, 2)), 'tile')]
    pallas_call x0 -> x2, Pallas kernels: none -> 95.3 us  [the longest x1 92.7 us: local(): pl.pallas_call(functools.partial(kernel, survey_n, tile_n), out_shape=jax...]
    ppermute x12 -> x0, starting transfers between devices: 47.7 us -> none  [the longest x6 32.9 us: extended(): before = lax.ppermute(last, axis, up)]
    scatter-add x4 -> x0, other arithmetic: 46.4 us -> none  [the longest x2 23.2 us: solve_round(): empty_sum.at[:, recv_index].add(denominator).reshape(3, rows_x, rows_y)]
    all_to_all x2 -> x0, waiting for transfers between devices: 33.6 us -> none  [send_traces(): lax.all_to_all(outgoing, 'survey', split_axis=0, concat_axis=0, tiled=True)]
    gather x4 -> x0, local copies, waits for them, and re-layouts: 30 us -> none  [the longest x2 15 us: solve_round(): own_rows = jnp.take(current, recv_index, axis=0)]
    reduce_sum x14 -> x0, other arithmetic: 20.5 us -> none  [the longest x2 18.4 us: pair_terms(): cross_term = jnp.mean(own_vals * partner_vals, axis=-1)]
    all_to_all x2 -> x0, starting transfers between devices: 15.3 us -> none  [send_traces(): lax.all_to_all(outgoing, 'survey', split_axis=0, concat_axis=0, tiled=True)]
  transfers between devices with their start and end apart: 14 -> 0, of which waited for: 6 -> 0; matrix products, arithmetic and copies ran while one was open for 5% -> 0% of each run, Pallas kernels for 0% -> 0%
where the time goes in v1:
time: 96.2 us; the launch traced here: 96 us
  Pallas kernels  95.3 us (99%)
    pallas_call x1, Pallas kernels, local(): pl.pallas_call(functools.partial(kernel, survey_n, tile_n), out_shape=jax...  92.7 us
    pallas_call x1, Pallas kernels, correct(): pl.pallas_call(correct_kernel, out_shape=(jax.ShapeDtypeStruct(fields.sha...  2.68 us

profile of v1, /device:TPU:6, one launch (start us, length us, event | category | flops | bytes accessed | tf_op | source)
XLA Modules:
  0.0 96.0 jit_solution(16191118762566073948)
XLA Ops:
  0.6 92.7 %shard_map.59.fields_hbm = f32[1,3,8,128]{3,2,1,0:T(8,128)} custom-call(bf16[1,8,128,256]{3,2,1,0:T(8,128)(2,1)} %data_hbm.3, s32[16,1,16,128]{3,2,1,0:T(8,128)} %index_hbm.1, s32[16,1,16]{2,1,0:T(1,128)} %count_hbm.1, f32[3]{0:T(128)} %strength_hbm.1), custom_call_target="tpu_custom_call" | custom-call | tf_op jit(solution)/shard_map/pallas_call | solution.py:407
  93.3 2.7 %shard_map.60 = (f32[1,3,8,128]{3,2,1,0:T(8,128)}, bf16[1,8,128,256]{3,2,1,0:T(8,128)(2,1)}) custom-call(bf16[1,8,128,256]{3,2,1,0:T(8,128)(2,1)} %data_hbm.3, f32[1,3,8,128]{3,2,1,0:T(8,128)} %shard_map.59.fields_hbm), custom_call_target="tpu_custom_call" | custom-call | tf_op jit(solution)/shard_map/pallas_call | solution.py:388

commit v2 on v1

--- a/solution.py
+++ b/solution.py
@@ -10,7 +10,8 @@
 ROUNDS = 2
 DAMPING = 0.05
 SIM_EPS = 1e-05
-CG_ITERS = 3
+SUMS = 2
+PIVOT = 3e-07
 CHUNK = 32
 LANES = 128
 F32 = jnp.float32
@@ -268,10 +269,12 @@
         power = lane1 % 8
 
         def powers(q):
-            return jnp.where(power == 1, q, 1.0) * jnp.where(power == 2, q * q, 1.0)
-
-        for step in range(CG_ITERS):
-            slot = r * CG_ITERS + step
+            once = (power == 1) | (power == 3) | (power == 5)
+            twice = (power == 2) | (power == 4) | (power == 5)
+            return jnp.where(once, q, 1.0) * jnp.where(twice, q * q, 1.0)
+
+        for step in range(SUMS):
+            slot = r * SUMS + step
             message = jnp.where(lane1 >= 64, 1.0, 0.0).astype(F32)
             images = []
             for c in range(3):
@@ -280,7 +283,12 @@
                 images.append(image)
                 p0, p1, q1 = residual[8:16], direction[8:16], image[8:16]
                 block = jnp.zeros((8, LANES), F32)
-                for k, (p, q) in enumerate(((p0, p0), (p1, q1), (q1, q1))):
+                pairs = [(p0, p0), (p1, q1), (q1, q1)]
+                if step == 1:
+                    pairs.append((p0, apply(residual, diagonal, off)[8:16]))
+                    again = apply(image, diagonal, off)[8:16]
+                    pairs += [(p0, again), (q1, again)]
+                for k, (p, q) in enumerate(pairs):
                     block = jnp.where(sub == k, jnp.sum(p * q, axis=0, keepdims=True), block)
                 sums = jnp.sum(block, axis=1, keepdims=True)
                 message = message + jnp.sum(jnp.where(lane == 8 * c + sub, sums, 0.0), axis=0, keepdims=True)
@@ -302,19 +310,24 @@
             m0 = jnp.zeros((1, LANES), F32)
             for d in range(tile_n):
                 m0 = m0 + rows[d] * powers(bounds[d] * inverse)
-            m1, m2 = [pltpu.roll(m0, LANES - k, 1) for k in (1, 2)]
+            m1, m2, m3, m4, m5 = [pltpu.roll(m0, LANES - k, 1) for k in range(1, 6)]
             alpha = m0 / m1
-            beta = jnp.maximum(alpha * alpha * m2 - m0, 0.0) / m0
+            fresh = jnp.maximum(alpha * alpha * m2 - m0, 0.0)
+            beta = fresh / m0
             along = alpha * inverse
             back = alpha * inverse * bounds[0]
+            scalars = [along, back, beta]
+            if step == 1:
+                pivot = m3 - 2.0 * alpha * m4 + alpha * alpha * m5 - beta * beta * m1
+                sound = pivot > PIVOT * m3
+                scalars.append(jnp.where(sound, fresh / jnp.where(sound, pivot, 1.0), 0.0) * inverse)
             for c in range(3):
-                k1, k2, k3 = [jnp.sum(jnp.where(lane1 == 8 * c, z, 0.0), axis=1, keepdims=True)
-                              for z in (along, back, beta)]
+                k = [jnp.sum(jnp.where(lane1 == 8 * c, z, 0.0), axis=1, keepdims=True) for z in scalars]
                 residual, direction, update = state[c][:3]
-                part = k1 * direction[8:16]
-                state[c][2] = part if step == 0 else update + part
-                state[c][0] = residual - k2 * images[c]
-                state[c][1] = state[c][0] + k3 * direction
+                part = k[0] * direction[8:16]
+                state[c][0] = residual - k[1] * images[c]
+                state[c][1] = state[c][0] + k[2] * direction
+                state[c][2] = part if step == 0 else update + part + k[3] * state[c][1][8:16]
         for c in range(3):
             fields_ref[0, c] = state[c][2] if r == 0 else fields_ref[0, c] + state[c][2]
 
@@ -339,8 +352,8 @@
     for r in range(ROUNDS):
         edge_copy(0, r).wait_send()
         edge_copy(1, r).wait_send()
-        for step in range(CG_ITERS):
-            moment_all(r * CG_ITERS + step).wait_send()
+        for step in range(SUMS):
+            moment_all(r * SUMS + step).wait_send()
 
 
 def correct_kernel(data_hbm, fields_hbm, fields_out, volume_hbm, data, fields, volume, load_sem, store_sem):
@@ -427,15 +440,15 @@
             pltpu.VMEM((ROUNDS, 6, rows_x, LANES), F32),
             pltpu.VMEM((ROUNDS, 6, rows_x, LANES), F32),
             pltpu.VMEM((ROUNDS, 6, rows_x, LANES), F32),
-            pltpu.VMEM((ROUNDS * CG_ITERS, 1, LANES), F32),
-            pltpu.VMEM((ROUNDS * CG_ITERS, tile_n, 1, LANES), F32),
+            pltpu.VMEM((ROUNDS * SUMS, 1, LANES), F32),
+            pltpu.VMEM((ROUNDS * SUMS, tile_n, 1, LANES), F32),
             pltpu.VMEM((rows_x, 8, LANES), F32),
             pltpu.VMEM((peers, 8, LANES), F32),
             pltpu.VMEM((peers, 8, LANES), F32),
             dma((5,)),
             dma((peers,)), dma((peers,)),
             dma((ROUNDS, 2)), dma((ROUNDS, 2)),
-            dma((ROUNDS * CG_ITERS,)), dma((ROUNDS * CG_ITERS,)),
+            dma((ROUNDS * SUMS,)), dma((ROUNDS * SUMS,)),
             dma((peers,)), dma((peers,)),
         ],
         compiler_params=pltpu.CompilerParams(

time: 96.2 us -> 84.9 us (0.88)
  Pallas kernels: 95.3 us -> 83.2 us
    pallas_call x1, Pallas kernels: 92.7 us -> 80.5 us  [local(): pl.pallas_call(functools.partial(kernel, survey_n, tile_n), out_shape=jax...]
where the time goes in v2:
time: 84.9 us; the launch traced here: 83.8 us
  Pallas kernels  83.2 us (98%)
    pallas_call x1, Pallas kernels, local(): pl.pallas_call(functools.partial(kernel, survey_n, tile_n), out_shape=jax...  80.5 us
    pallas_call x1, Pallas kernels, correct(): pl.pallas_call(correct_kernel, out_shape=(jax.ShapeDtypeStruct(fields.sha...  2.68 us

profile of v2, /device:TPU:6, one launch (start us, length us, event | category | flops | bytes accessed | tf_op | source)
XLA Modules:
  0.0 83.8 jit_solution(614554219368832473)
XLA Ops:
  0.6 80.5 %shard_map.59.fields_hbm = f32[1,3,8,128]{3,2,1,0:T(8,128)} custom-call(bf16[1,8,128,256]{3,2,1,0:T(8,128)(2,1)} %data_hbm.3, s32[16,1,16,128]{3,2,1,0:T(8,128)} %index_hbm.1, s32[16,1,16]{2,1,0:T(1,128)} %count_hbm.1, f32[3]{0:T(128)} %strength_hbm.1), custom_call_target="tpu_custom_call" | custom-call | tf_op jit(solution)/shard_map/pallas_call | solution.py:420
  81.1 2.7 %shard_map.60 = (f32[1,3,8,128]{3,2,1,0:T(8,128)}, bf16[1,8,128,256]{3,2,1,0:T(8,128)(2,1)}) custom-call(bf16[1,8,128,256]{3,2,1,0:T(8,128)(2,1)} %data_hbm.3, f32[1,3,8,128]{3,2,1,0:T(8,128)} %shard_map.59.fields_hbm), custom_call_target="tpu_custom_call" | custom-call | tf_op jit(solution)/shard_map/pallas_call | solution.py:401

commit v3 on v1

--- a/solution.py
+++ b/solution.py
@@ -204,7 +204,7 @@
         x0 = start // LANES
         y0 = start % LANES
         x1 = jnp.minimum(x0 + 1, rows_x - 1)
-        field_out[j] = jnp.where(lane >= y0, field_rows[x0], field_rows[x1])
+        field_out[j] = jnp.where(lane[0:4] >= y0, field_rows[x0], field_rows[x1])
         field_copy(j).start()
         return c
 
@@ -324,7 +324,7 @@
     for x in range(rows_x):
         for c in range(3):
             field_rows[x, c:c + 1, :] = fields_ref[0, c, x:x + 1, :]
-        field_rows[x, 3:8, :] = jnp.zeros((5, LANES), F32)
+        field_rows[x, 3:4, :] = jnp.zeros((1, LANES), F32)
     lax.fori_loop(0, peers, send_fields, 0)
     lax.fori_loop(0, rows_x, later_own, 0)
     carry = lax.fori_loop(0, peers, later_list, (zero,) * 4)
@@ -429,9 +429,9 @@
             pltpu.VMEM((ROUNDS, 6, rows_x, LANES), F32),
             pltpu.VMEM((ROUNDS * CG_ITERS, 1, LANES), F32),
             pltpu.VMEM((ROUNDS * CG_ITERS, tile_n, 1, LANES), F32),
-            pltpu.VMEM((rows_x, 8, LANES), F32),
-            pltpu.VMEM((peers, 8, LANES), F32),
-            pltpu.VMEM((peers, 8, LANES), F32),
+            pltpu.VMEM((rows_x, 4, LANES), F32),
+            pltpu.VMEM((peers, 4, LANES), F32),
+            pltpu.VMEM((peers, 4, LANES), F32),
             dma((5,)),
             dma((peers,)), dma((peers,)),
             dma((ROUNDS, 2)), dma((ROUNDS, 2)),

time: 96.2 us -> 96.2 us (level)
  no operation moved by 1% of the time
where the time goes in v3:
time: 96.2 us; the launch traced here: 95.9 us
  Pallas kernels  95.3 us (99%)
    pallas_call x1, Pallas kernels, local(): pl.pallas_call(functools.partial(kernel, survey_n, tile_n), out_shape=jax...  92.6 us
    pallas_call x1, Pallas kernels, correct(): pl.pallas_call(correct_kernel, out_shape=(jax.ShapeDtypeStruct(fields.sha...  2.68 us

profile of v3, /device:TPU:6, one launch (start us, length us, event | category | flops | bytes accessed | tf_op | source)
XLA Modules:
  0.0 95.9 jit_solution(6960750643717696665)
XLA Ops:
  0.6 92.6 %shard_map.59.fields_hbm = f32[1,3,8,128]{3,2,1,0:T(8,128)} custom-call(bf16[1,8,128,256]{3,2,1,0:T(8,128)(2,1)} %data_hbm.3, s32[16,1,16,128]{3,2,1,0:T(8,128)} %index_hbm.1, s32[16,1,16]{2,1,0:T(1,128)} %count_hbm.1, f32[3]{0:T(128)} %strength_hbm.1), custom_call_target="tpu_custom_call" | custom-call | tf_op jit(solution)/shard_map/pallas_call | solution.py:407
  93.3 2.7 %shard_map.60 = (f32[1,3,8,128]{3,2,1,0:T(8,128)}, bf16[1,8,128,256]{3,2,1,0:T(8,128)(2,1)}) custom-call(bf16[1,8,128,256]{3,2,1,0:T(8,128)(2,1)} %data_hbm.3, f32[1,3,8,128]{3,2,1,0:T(8,128)} %shard_map.59.fields_hbm), custom_call_target="tpu_custom_call" | custom-call | tf_op jit(solution)/shard_map/pallas_call | solution.py:388
